TPU v7x, 32 devices: a whole 2x2x4 slice. The times are simulated.
32 devices in a mesh: row: 4 (over z), col: 8 (over y, x, core).
Axes of the slice: x: 2, y: 2, z: 4, core: 2. Of those that a mesh axis runs over, the one named last changes fastest.
Arguments:
- base_matrix: float32 [4096, 4096], P('row', 'col')
- inverse_factors: bfloat16 [128, 2, 512, 512], P(('row', 'col')), may hold values from -0.26516504 to 0.26516504
- coupling: bfloat16 [128, 2, 512, 256], P(('row', 'col')), may hold values from -0.36 to 0.36
- positions: int32 [128, 256], P(('row', 'col')), may hold values from 0 to 127, as said below
- counts: int32 [128, 4], P(('row', 'col')), may hold values from 1 to 64, as said below
- owners: int32 [128], P(('row', 'col')), may hold values from 0 to 7, as said below
Outputs:
- factored: float32 [4096, 4096], P('row', 'col')
Inputs may be any that keep to these rules, and one draw needn't show every extreme that they name: Within each partition and each slot group of 64 slots, positions are distinct. `counts`: in every partition at least one slot group is fully used. `owners`: among the partitions held by the devices of one index of col, at most 4 share an owner, and exactly 4 do for some owner.
All inputs are finite; a program needn't handle non-finite values.
Results may differ from a plain program's by a relative error of at most 0.0003.
Values sent between devices are 32-bit elements; how exact they have to be, the bound alone decides.
A program may use at most 128 MiB of HBM per device.

v0:
```python
import jax
import jax.numpy as jnp
from jax import lax
from jax.sharding import PartitionSpec as P

TILE = 128
KS = 256
MOST = 4


def spread(value, axis, root):
    mine = lax.axis_index(axis) == root
    return lax.psum(jnp.where(mine, value, jnp.zeros_like(value)), axis)


def local(base_matrix, inverse_factors, coupling, positions, counts, owners):
    rows_dev, cols_dev = base_matrix.shape
    row_count = lax.axis_size("row")
    col_count = lax.axis_size("col")
    row_index = lax.axis_index("row")
    col_index = lax.axis_index("col")
    part_dev = coupling.shape[0]
    slot_width = KS // row_count
    factor = jnp.einsum(
        "pbij,pbjk->pbik", inverse_factors, coupling, preferred_element_type=jnp.float32
    ).astype(jnp.bfloat16)
    schur_rows = jnp.einsum("pbik,pbil->pkl", factor, factor, preferred_element_type=jnp.float32)
    slot_group = jnp.arange(KS, dtype=jnp.int32) // slot_width
    within = jnp.arange(KS, dtype=jnp.int32) % slot_width
    group_match = (slot_group[None, :] == jnp.arange(row_count, dtype=jnp.int32)[:, None]).astype(
        jnp.int32
    )
    limits = jnp.sum(counts[:, :, None] * group_match[None, :, :], axis=1)
    usable = (within[None, :] < limits).astype(jnp.float32)
    schur_rows = schur_rows * usable[:, :, None] * usable[:, None, :]
    unknown = owners[:, None] * cols_dev + slot_group[None, :] * TILE + positions
    pieces = schur_rows.reshape(part_dev, row_count, slot_width, KS)
    labels = jnp.broadcast_to(unknown[:, None, :], (part_dev, row_count, KS))
    received, received_labels = (
        lax.all_to_all(pieces, "row", split_axis=1, concat_axis=1, tiled=True),
        lax.all_to_all(labels, "row", split_axis=1, concat_axis=1, tiled=True),
    )
    item_total = part_dev * row_count
    arrived_items = received.reshape(item_total, slot_width, KS)
    item_labels = received_labels.reshape(item_total, KS)
    target = item_labels[:, 0] // cols_dev
    shared = target[:, None] == target[None, :]
    earlier = jnp.arange(item_total)[None, :] < jnp.arange(item_total)[:, None]
    order_rank = jnp.sum((shared & earlier).astype(jnp.int32), axis=1)
    chooser = (target[None, None, :] == jnp.arange(col_count, dtype=jnp.int32)[:, None, None]) & (
        order_rank[None, None, :] == jnp.arange(MOST, dtype=jnp.int32)[None, :, None]
    )
    outgoing = jnp.einsum(
        "csm,mxy->csxy", chooser.astype(jnp.float32), arrived_items, precision=lax.Precision.HIGHEST
    )
    outgoing_labels = jnp.einsum("csm,my->csy", chooser.astype(jnp.int32), item_labels)
    landed, landed_labels = (
        lax.all_to_all(outgoing, "col", split_axis=0, concat_axis=0, tiled=True),
        lax.all_to_all(outgoing_labels, "col", split_axis=0, concat_axis=0, tiled=True),
    )
    landed_total = landed.shape[0] * landed.shape[1]
    tile_slots = jnp.arange(TILE, dtype=jnp.int32)
    row_labels = (
        lax.dynamic_slice_in_dim(landed_labels, row_index * slot_width, slot_width, 2) % TILE
    )
    row_labels = row_labels.reshape(landed_total, slot_width)
    row_onehot = (row_labels[:, :, None] == tile_slots[None, None, :]).astype(jnp.float32)
    col_labels = (landed_labels % TILE).reshape(landed_total, row_count, slot_width)
    col_onehot = (col_labels[:, :, :, None] == tile_slots[None, None, None, :]).astype(jnp.float32)
    landed_items = landed.reshape(landed_total, slot_width, row_count, slot_width)
    spread_cols = jnp.einsum(
        "isgk,igkt->isgt", landed_items, col_onehot, precision=lax.Precision.HIGHEST
    )
    spread_cols = spread_cols.reshape(landed_total, slot_width, cols_dev)
    accumulated = jnp.einsum(
        "isr,isc->rc", row_onehot, spread_cols, precision=lax.Precision.HIGHEST
    )
    row_start = col_index * TILE
    current = lax.dynamic_slice_in_dim(base_matrix, row_start, TILE, 0)
    assembled = lax.dynamic_update_slice_in_dim(base_matrix, current - accumulated, row_start, 0)
    local_rows = jnp.arange(rows_dev, dtype=jnp.int32)
    row_unknown = (local_rows // TILE * row_count + row_index) * TILE + local_rows % TILE

    def panel(column_block, panel_index):
        diagonal = spread(column_block[:TILE], "row", panel_index)
        lower = jnp.linalg.cholesky(diagonal)
        identity = jnp.eye(TILE, dtype=jnp.float32)
        inverse = lax.linalg.triangular_solve(lower, identity, left_side=True, lower=True)
        solved = jnp.dot(
            column_block,
            inverse.T,
            precision=lax.Precision.HIGHEST,
            preferred_element_type=jnp.float32,
        )
        tile_values = jnp.tile(lower, (rows_dev // TILE, 1))
        in_tile = row_unknown // TILE == panel_index
        below = row_unknown >= (panel_index + 1) * TILE
        rows_part = jnp.where(
            in_tile[:, None], tile_values, jnp.where(below[:, None], solved, jnp.zeros_like(solved))
        )
        rows_part = spread(rows_part, "col", 0)
        own_tile = lax.dynamic_slice_in_dim(rows_part, col_index * TILE, TILE, 0)
        cols_part = lax.all_gather(own_tile, "row", axis=0, tiled=True)
        return (rows_part, cols_part)

    first_rows, first_cols = panel(assembled[:, :TILE], 0)
    updated = assembled - jnp.dot(
        first_rows,
        first_cols.T,
        precision=lax.Precision.HIGHEST,
        preferred_element_type=jnp.float32,
    )
    second_rows, second_cols = panel(updated[:, TILE : 2 * TILE], 1)
    trailing = updated - jnp.dot(
        second_rows,
        second_cols.T,
        precision=lax.Precision.HIGHEST,
        preferred_element_type=jnp.float32,
    )
    col_unknown = col_index * cols_dev + jnp.arange(cols_dev, dtype=jnp.int32)
    leading = jnp.concatenate(
        [first_rows, second_rows, jnp.zeros((rows_dev, cols_dev - 2 * TILE), jnp.float32)], axis=1
    )
    blank = (row_unknown < 2 * TILE)[:, None]
    rest = jnp.where(blank, jnp.zeros_like(trailing), trailing)
    return jnp.where((col_unknown < 2 * TILE)[None, :], leading, rest)


def solution(mesh):
    in_specs = (
        P("row", "col"),
        P(("row", "col"), None, None, None),
        P(("row", "col"), None, None, None),
        P(("row", "col"), None),
        P(("row", "col"), None),
        P(("row", "col")),
    )
    out_specs = P("row", "col")
    return jax.shard_map(local, mesh=mesh, in_specs=in_specs, out_specs=out_specs, check_vma=False)
```

profile of v0, /device:TPU:0, one launch (start us, length us, event | category | flops | bytes accessed | tf_op | source)
XLA Modules:
  0.0 390.6 jit_solution(18383805007004442810)
XLA Ops:
  8.7 6.3 %all-to-all-start = ((s32[4,4,256]{2,0,1:T(4,128)}), s32[4,4,256]{2,0,1:T(4,128)S(1)}, u32[]{:S(2)}, u32[]{:S(2)}) async-start(s32[4,4,256]{2,0,1:T(4,128)} %broadcast_in_dim.45), calls=%async_computation | async-start | bytes 32768 | tf_op jit(solution)/shard_map/all_to_all | solution.py:41
  15.8 6.4 %fusion.19 = f32[4,256,256]{2,1,0:T(8,128)S(1)} fusion(bf16[4,2,512,512]{3,2,1,0:T(8,128)(2,1)} %param.10, bf16[4,2,512,256]{3,2,1,0:T(8,128)(2,1)S(1)} %copy-done, f32[4,256]{1,0:T(4,128)S(1)} %compare_convert_fusion), kind=kOutput, calls=%fused_computation.15 | convolution fusion | flops 1612185600 | bytes 7344128 | tf_op jit(solution)/shard_map/pbik,pbil->pkl/dot_general | solution.py:27
  23.3 5.1 %all-to-all-start.2 = ((f32[4,4,64,256]{3,2,0,1:T(8,128)}), f32[4,4,64,256]{3,2,0,1:T(8,128)S(1)}, u32[]{:S(2)}, u32[]{:S(2)}) async-start(f32[4,4,64,256]{3,2,0,1:T(8,128)} %copy.64), calls=%async_computation.2 | async-start | bytes 2097152 | tf_op jit(solution)/shard_map/all_to_all | solution.py:40
  29.5 24.0 %all-to-all-done.2 = f32[4,4,64,256]{3,2,0,1:T(8,128)S(1)} async-done(((f32[4,4,64,256]{3,2,0,1:T(8,128)}), f32[4,4,64,256]{3,2,0,1:T(8,128)S(1)}, u32[]{:S(2)}, u32[]{:S(2)}) %all-to-all-start.2) | async-done | bytes 1048608 | tf_op jit(solution)/shard_map/all_to_all | solution.py:40
  53.5 3.7 all-to-all-start.1
  63.5 4.3 %all-to-all-start.3 = ((f32[8,4,64,256]{3,2,1,0:T(8,128)}), f32[8,4,64,256]{3,2,1,0:T(8,128)}, u32[]{:S(2)}, u32[]{:S(2)}) async-start(f32[8,4,64,256]{3,2,1,0:T(8,128)} %copy.66), calls=%async_computation.3 | async-start | bytes 4194304 | tf_op jit(solution)/shard_map/all_to_all | solution.py:58
  68.1 2.9 copy.70
  71.2 23.3 %all-to-all-done.3 = f32[8,4,64,256]{3,2,1,0:T(8,128)} async-done(((f32[8,4,64,256]{3,2,1,0:T(8,128)}), f32[8,4,64,256]{3,2,1,0:T(8,128)}, u32[]{:S(2)}, u32[]{:S(2)}) %all-to-all-start.3) | async-done | bytes 2097184 | tf_op jit(solution)/shard_map/all_to_all | solution.py:58
  94.5 5.1 %reshape.281 = f32[32,64,4,64]{3,2,1,0:T(4,128)} reshape(f32[8,4,64,256]{3,2,1,0:T(8,128)} %all-to-all-done.3) | data formatting | bytes 4194304 | tf_op jit(solution)/shard_map/reshape | solution.py:70
  99.6 5.0 %fusion.5 = f32[32,4,8,8,128]{4,3,2,1,0:T(8,128)S(1)} fusion(f32[32,64,4,64]{3,2,1,0:T(4,128)} %reshape.281, s32[32,4,64]{2,1,0:T(4,128)S(1)} %eq.155), kind=kOutput, calls=%fused_computation.6 | convolution fusion | flops 806354944 | bytes 6324224 | tf_op jit(solution)/shard_map/isgk,igkt->isgt/dot_general | solution.py:71
  104.6 5.4 %fusion.32 = f32[1024,512]{0,1:T(8,128)} fusion(f32[1024,512]{0,1:T(8,128)} %copy.70, s32[]{:T(128)S(6)} %select_n.171, f32[32,4,8,8,128]{4,3,2,1,0:T(8,128)S(1)} %fusion.5, s32[32,64]{1,0:T(8,128)S(1)} %bitcast.77), kind=kOutput, calls=%fused_computation.24 | convolution fusion | flops 1610940416 | bytes 4726788 | tf_op jit(solution)/shard_map/isr,isc->rc/dot_general | solution.py:75
  111.7 31.1 %all-reduce.5.cloned.1.call-done = f32[128,128]{0,1:T(8,128)} async-done(((f32[128,128]{0,1:T(8,128)}), f32[128,128]{0,1:T(8,128)}) %all-reduce.5.cloned.1.call-update) | async-done | bytes 65552 | tf_op jit(solution)/shard_map/psum | solution.py:13
  144.6 11.7 %cholesky.44 = f32[128,128]{1,0:T(8,128)S(1)} custom-call(f32[128,128]{1,0:T(8,128)S(1)} %fusion.45), custom_call_target="Cholesky" | custom-call | tf_op jit(solution)/shard_map/jit(cholesky)/cholesky | solution.py:86
  157.9 9.8 %custom-call.6 = f32[1,128,128]{1,2,0:T(8,128)S(1)} custom-call(f32[1,128,128]{2,1,0:T(8,128)S(1)} %get-tuple-element.11), custom_call_target="InvertDiagBlocksLowerTriangular" | custom-call | tf_op jit(solution)/shard_map/triangular_solve/custom-call.0 | solution.py:88
  170.7 54.3 %all-reduce.7.cloned.1.call-done = f32[1024,128]{0,1:T(8,128)} async-done(((f32[1024,128]{0,1:T(8,128)}), f32[1024,128]{0,1:T(8,128)}) %all-reduce.7.cloned.1.call-update) | async-done | bytes 524304 | tf_op jit(solution)/shard_map/psum | solution.py:13
  225.9 13.9 %all_gather.6 = f32[512,128]{0,1:T(8,128)S(1)} all-gather(f32[128,128]{0,1:T(8,128)S(1)} %constant_dynamic-slice_fusion), channel_id=1, replica_groups=mesh['row'=4,'col'=8] {'row'}, dimensions={0}, use_global_device_ids=true | all-gather | bytes 327680 | tf_op jit(solution)/shard_map/all_gather | solution.py:103
  239.8 3.6 convolution_subtract_fusion
  245.7 33.1 %all-reduce.9.cloned.1.call-done = f32[128,128]{0,1:T(8,128)} async-done(((f32[128,128]{0,1:T(8,128)}), f32[128,128]{0,1:T(8,128)}) %all-reduce.9.cloned.1.call-update) | async-done | bytes 65552 | tf_op jit(solution)/shard_map/psum | solution.py:13
  280.6 11.7 %cholesky.55 = f32[128,128]{1,0:T(8,128)S(1)} custom-call(f32[128,128]{1,0:T(8,128)S(1)} %fusion.43), custom_call_target="Cholesky" | custom-call | tf_op jit(solution)/shard_map/jit(cholesky)/cholesky | solution.py:86
  293.9 9.8 %custom-call.7 = f32[1,128,128]{1,2,0:T(8,128)S(1)} custom-call(f32[1,128,128]{2,1,0:T(8,128)S(1)} %get-tuple-element.9), custom_call_target="InvertDiagBlocksLowerTriangular" | custom-call | tf_op jit(solution)/shard_map/triangular_solve/custom-call.0 | solution.py:88
  306.7 54.3 %all-reduce.11.cloned.1.call-done = f32[1024,128]{0,1:T(8,128)} async-done(((f32[1024,128]{0,1:T(8,128)}), f32[1024,128]{0,1:T(8,128)}) %all-reduce.11.cloned.1.call-update) | async-done | bytes 524304 | tf_op jit(solution)/shard_map/psum | solution.py:13
  361.9 13.9 %all_gather.7 = f32[512,128]{0,1:T(8,128)S(1)} all-gather(f32[128,128]{0,1:T(8,128)S(1)} %constant_dynamic-slice_fusion.1), channel_id=1, replica_groups=mesh['row'=4,'col'=8] {'row'}, dimensions={0}, use_global_device_ids=true | all-gather | bytes 327680 | tf_op jit(solution)/shard_map/all_gather | solution.py:103
  375.8 5.4 %maximum_select_fusion = f32[1024,512]{0,1:T(8,128)} fusion(f32[1024,128]{0,1:T(8,128)} %all-reduce.11.cloned.1.call-done, f32[1024,128]{0,1:T(8,128)S(1)} %copy-done.2, f32[1024,512]{0,1:T(8,128)} %copy-done.1, f32[512,128]{0,1:T(8,128)S(1)} %all_gather.7, f32[512]{0:T(512)S(1)} %pad.2.clone, pred[512]{0:T(512)(128)(4,1)S(1)} %add_compare_fusion, ...), kind=kOutput, calls=%fused_computation.7 | convolution fusion | flops 807927808 | bytes 5508608 | tf_op jit(solution)/shard_map/dot_general | solution.py:114
  381.2 2.9 copy.79
  (70 shorter events, 30.0 us)
Async XLA Ops:
  6.5 9.3 %copy-start = (bf16[4,2,512,256]{3,2,1,0:T(8,128)(2,1)S(1)}, bf16[4,2,512,256]{3,2,1,0:T(8,128)(2,1)}, u32[]{:S(2)}) copy-start(bf16[4,2,512,256]{3,2,1,0:T(8,128)(2,1)} %param.11) | copy-start | bytes 6291460
  8.7 14.6 %all-to-all-start = ((s32[4,4,256]{2,0,1:T(4,128)}), s32[4,4,256]{2,0,1:T(4,128)S(1)}, u32[]{:S(2)}, u32[]{:S(2)}) async-start(s32[4,4,256]{2,0,1:T(4,128)} %broadcast_in_dim.45), calls=%async_computation | async-start | bytes 32768 | tf_op jit(solution)/shard_map/all_to_all | solution.py:41
  23.3 30.3 %all-to-all-start.2 = ((f32[4,4,64,256]{3,2,0,1:T(8,128)}), f32[4,4,64,256]{3,2,0,1:T(8,128)S(1)}, u32[]{:S(2)}, u32[]{:S(2)}) async-start(f32[4,4,64,256]{3,2,0,1:T(8,128)} %copy.64), calls=%async_computation.2 | async-start | bytes 2097152 | tf_op jit(solution)/shard_map/all_to_all | solution.py:40
  53.5 9.9 %all-to-all-start.1 = ((s32[8,4,256]{2,1,0:T(4,128)}), s32[8,4,256]{2,1,0:T(4,128)S(1)}, u32[]{:S(2)}, u32[]{:S(2)}) async-start(s32[8,4,256]{2,1,0:T(4,128)} %fusion.50), calls=%async_computation.1 | async-start | bytes 65536 | tf_op jit(solution)/shard_map/all_to_all | solution.py:59
  63.5 31.0 %all-to-all-start.3 = ((f32[8,4,64,256]{3,2,1,0:T(8,128)}), f32[8,4,64,256]{3,2,1,0:T(8,128)}, u32[]{:S(2)}, u32[]{:S(2)}) async-start(f32[8,4,64,256]{3,2,1,0:T(8,128)} %copy.66), calls=%async_computation.3 | async-start | bytes 4194304 | tf_op jit(solution)/shard_map/all_to_all | solution.py:58
  67.8 75.0 %all-reduce.5.cloned.1.call-start = ((), (), s32[]{:S(2)}) async-start(), calls=%async_computation.4 | async-start | bytes 131072 | tf_op jit(solution)/shard_map/psum | solution.py:13
  111.5 113.6 %all-reduce.7.cloned.1.call-start = ((), (), s32[]{:S(2)}) async-start(), calls=%async_computation.5 | async-start | bytes 1048576 | tf_op jit(solution)/shard_map/psum | solution.py:13
  170.6 108.2 %all-reduce.9.cloned.1.call-start = ((), (), s32[]{:S(2)}) async-start(), calls=%async_computation.6 | async-start | bytes 131072 | tf_op jit(solution)/shard_map/psum | solution.py:13
  243.4 1.3 copy-start.1
  245.4 130.4 %copy-start.2 = (f32[1024,128]{0,1:T(8,128)S(1)}, f32[1024,128]{0,1:T(8,128)}, u32[]{:S(2)}) copy-start(f32[1024,128]{0,1:T(8,128)} %all-reduce.7.cloned.1.call-done) | copy-start | bytes 1572868
  245.4 115.6 %all-reduce.11.cloned.1.call-start = ((), (), s32[]{:S(2)}) async-start(), calls=%async_computation.7 | async-start | bytes 1048576 | tf_op jit(solution)/shard_map/psum | solution.py:13
Sparse Core Ops, SparseCore 0:
  111.6 31.2 all-reduce.4
  170.8 54.2 all-reduce.6
  245.5 33.2 all-reduce.8
  306.7 54.2 all-reduce.10
where the time goes:
time: 392 us; the launch traced here: 391 us
  waiting for transfers between devices  220 us (56%)
  other arithmetic  52.6 us (13%)
  matrix products  33.2 us (8%)
  blocking collectives  27.9 us (7%)
  local copies, waits for them, and re-layouts  23 us (6%)
  starting transfers between devices  20.3 us (5%)
  between operations  13.4 us (3%)
    psum x4, waiting for transfers between devices, spread(): return lax.psum(jnp.where(mine, value, jnp.zeros_like(value)), axis)  173 us
    all_gather x2, blocking collectives, panel(): cols_part = lax.all_gather(own_tile, 'row', axis=0, tiled=True)  27.9 us
    another operation x6, other arithmetic, panel(): lower = jnp.linalg.cholesky(diagonal)  24.9 us
    all_to_all x1, waiting for transfers between devices, local(): lax.all_to_all(pieces, 'row', split_axis=1, concat_axis=1, tiled=True)  24 us
    all_to_all x1, waiting for transfers between devices, local(): lax.all_to_all(outgoing, 'col', split_axis=0, concat_axis=0, tiled=True)  23.3 us
    another operation x4, other arithmetic, panel(): lax.linalg.triangular_solve(lower, identity, left_side=True, lower=True)  21 us
  transfers between devices with their start and end apart: 8, of which 6 were waited for; matrix products, arithmetic and copies ran while one was open for 5% of the time, Pallas kernels for 0%

commit v1 on v0

v1 whole, which is shorter than its diff:
```python
import functools

import jax
import jax.numpy as jnp
from jax import lax
from jax.experimental import pallas as pl
from jax.experimental.pallas import tpu as pltpu
from jax.sharding import PartitionSpec as P

TILE = 128
KS = 256
PANEL = 2 * TILE
VMEM_BYTES = 50 * 1024 * 1024
MESH = pl.DeviceIdType.MESH
NT = (((1,), (1,)), ((), ()))
NN = (((1,), (0,)), ((), ()))


def exchange_kernel(
    n_row,
    n_col,
    part_dev,
    base_ref,
    pieces_ref,
    labels_ref,
    raw_ref,
    q_ref,
    diag_ref,
    top_ref,
    tile_ref,
    got,
    got_labels,
    wide_hi,
    wide_lo,
    partial,
    landed,
    piece_send,
    piece_recv,
    label_send,
    label_recv,
    raw_send,
    raw_recv,
    q_send,
    q_recv,
    part_send,
    part_recv,
    diag_send,
    diag_recv,
    top_send,
    top_recv,
    local_sem,
):
    r = lax.axis_index("row")
    c = lax.axis_index("col")
    width = KS // n_row
    cols_dev = n_row * TILE

    def row_peer(d):
        return lax.rem(r + d, n_row)

    def row_source(d):
        return lax.rem(r + n_row - d, n_row)

    def col_peer(d):
        return lax.rem(c + d, n_col)

    def col_source(d):
        return lax.rem(c + n_col - d, n_col)

    barrier = pltpu.get_barrier_semaphore()
    for d in range(1, n_row):
        pl.semaphore_signal(barrier, inc=1, device_id={"row": row_peer(d)}, device_id_type=MESH)
    for d in range(1, n_col):
        pl.semaphore_signal(barrier, inc=1, device_id={"col": col_peer(d)}, device_id_type=MESH)
    pl.semaphore_wait(barrier, n_row + n_col - 2)

    def piece_copy(to, slot):
        return pltpu.make_async_remote_copy(
            src_ref=pieces_ref.at[to],
            dst_ref=got.at[slot],
            send_sem=piece_send.at[to],
            recv_sem=piece_recv.at[slot],
            device_id={"row": to},
            device_id_type=MESH,
        )

    def label_copy(to, slot):
        return pltpu.make_async_remote_copy(
            src_ref=labels_ref.at[to],
            dst_ref=got_labels.at[slot],
            send_sem=label_send.at[to],
            recv_sem=label_recv.at[slot],
            device_id={"row": to},
            device_id_type=MESH,
        )

    def raw_copy(to):
        return pltpu.make_async_remote_copy(
            src_ref=base_ref.at[:, pl.ds(0, PANEL)],
            dst_ref=raw_ref,
            send_sem=raw_send.at[to],
            recv_sem=raw_recv,
            device_id={"col": to},
            device_id_type=MESH,
        )

    def q_copy(to, half):
        return pltpu.make_async_remote_copy(
            src_ref=q_ref.at[pl.ds(half * TILE, TILE)],
            dst_ref=q_ref.at[pl.ds(half * TILE, TILE)],
            send_sem=q_send.at[to],
            recv_sem=q_recv.at[half],
            device_id={"row": to},
            device_id_type=MESH,
        )

    def part_copy(to, slot):
        return pltpu.make_async_remote_copy(
            src_ref=partial.at[to],
            dst_ref=landed.at[slot],
            send_sem=part_send.at[to],
            recv_sem=part_recv.at[slot],
            device_id={"col": to},
            device_id_type=MESH,
        )

    def diag_copy(to):
        return pltpu.make_async_remote_copy(
            src_ref=diag_ref,
            dst_ref=diag_ref,
            send_sem=diag_send.at[to],
            recv_sem=diag_recv,
            device_id={"col": to},
            device_id_type=MESH,
        )

    def top_copy(to):
        return pltpu.make_async_remote_copy(
            src_ref=top_ref,
            dst_ref=top_ref,
            send_sem=top_send.at[to],
            recv_sem=top_recv,
            device_id={"col": to},
            device_id_type=MESH,
        )

    for d in range(1, n_row):
        label_copy(row_peer(d), r).start()
    for d in range(1, n_row):
        piece_copy(row_peer(d), r).start()
    own_piece = pltpu.make_async_copy(pieces_ref.at[r], got.at[r], local_sem.at[0])
    own_label = pltpu.make_async_copy(labels_ref.at[r], got_labels.at[r], local_sem.at[1])
    own_piece.start()
    own_label.start()

    @pl.when(c == 0)
    def _():
        for to in range(1, n_col):
            raw_copy(to).start()
        own_raw = pltpu.make_async_copy(
            base_ref.at[:, pl.ds(0, PANEL)], raw_ref, local_sem.at[2]
        )
        own_raw.start()
        own_raw.wait()

    own_tile = pltpu.make_async_copy(
        base_ref.at[pl.ds(c * TILE, TILE)], tile_ref, local_sem.at[3]
    )
    own_tile.start()

    own_piece.wait()
    own_label.wait()

    def widen(src):
        for p in range(part_dev):
            block = got[src, pl.ds(p * width, width), :]
            high = block.astype(jnp.bfloat16)
            low = (block - high.astype(jnp.float32)).astype(jnp.bfloat16)
            code = got_labels[src, pl.ds(p, 1), :]
            spot = lax.broadcasted_iota(jnp.int32, (cols_dev, KS), 0)
            onehot = jnp.where(spot == code, 1.0, 0.0).astype(jnp.bfloat16)
            both = jnp.concatenate([high, low], axis=0)
            out = lax.dot_general(both, onehot, NT, preferred_element_type=jnp.float32)
            out = out.astype(jnp.bfloat16)
            wide_hi[src, pl.ds(p * width, width), :] = out[:width]
            wide_lo[src, pl.ds(p * width, width), :] = out[width:]

    widen(r)

    def arrive(d, carry):
        src = lax.rem(r + n_row - d, n_row)
        label_copy(row_peer(1), src).wait_recv()
        piece_copy(row_peer(1), src).wait_recv()
        widen(src)
        return carry

    lax.fori_loop(1, n_row, arrive, 0)

    def send_q(half):
        for d in range(1, n_row):
            q_copy(row_peer(d), half).start()

    for half in range(2):

        @pl.when((r == half) & (c != 0))
        def _():
            own_q = pltpu.make_async_copy(
                base_ref.at[pl.ds(0, TILE)], q_ref.at[pl.ds(half * TILE, TILE)], local_sem.at[4]
            )
            own_q.start()
            own_q.wait()
            send_q(half)

    def gather_owner(o, carry):
        total = jnp.zeros((TILE, cols_dev), jnp.float32)
        for src in range(n_row):
            code = got_labels[src, pl.ds(part_dev, 1), :][:, : part_dev * width]
            spot = lax.broadcasted_iota(jnp.int32, (TILE, part_dev * width), 0) + o * TILE
            onehot = jnp.where(spot == code, 1.0, 0.0).astype(jnp.bfloat16)
            total += lax.dot_general(onehot, wide_hi[src], NN, preferred_element_type=jnp.float32)
            total += lax.dot_general(onehot, wide_lo[src], NN, preferred_element_type=jnp.float32)
        partial[o] = total

        @pl.when(o != c)
        def _():
            part_copy(o, c).start()

        return carry

    lax.fori_loop(0, n_col, gather_owner, 0)

    own_tile.wait()
    summed = partial[c]
    for d in range(1, n_col):
        src = col_source(d)
        part_copy(col_peer(1), src).wait_recv()
        summed += landed[src]
    tile_ref[...] = tile_ref[...] - summed

    for half in range(2):

        @pl.when((r == half) & (c == 0))
        def _():
            q_ref[pl.ds(half * TILE, TILE), :] = tile_ref[...]
            send_q(half)

    @pl.when(c == 0)
    def _():
        top_ref[...] = tile_ref[:, :PANEL]

    for half in range(2):

        @pl.when(r != half)
        def _():
            q_copy(row_peer(1), half).wait_recv()

    @pl.when(c == 0)
    def _():
        diag_ref[...] = q_ref[:, :PANEL]
        for to in range(1, n_col):
            diag_copy(to).start()
        for to in range(1, n_col):
            top_copy(to).start()

    @pl.when(c != 0)
    def _():
        diag_copy(0).wait_recv()
        top_copy(0).wait_recv()
        raw_copy(0).wait_recv()

    @pl.when(c == 0)
    def _():
        for to in range(1, n_col):
            diag_copy(to).wait_send()
            top_copy(to).wait_send()
            raw_copy(to).wait_send()

    for d in range(1, n_row):
        label_copy(row_peer(d), r).wait_send()
        piece_copy(row_peer(d), r).wait_send()
    for d in range(1, n_col):
        part_copy(col_peer(d), c).wait_send()
    for half in range(2):

        @pl.when(r == half)
        def _():
            for d in range(1, n_row):
                q_copy(row_peer(d), half).wait_send()


def exchange(n_row, n_col, base, pieces, labels):
    rows_dev, cols_dev = base.shape
    part_dev = pieces.shape[1] // (KS // n_row)
    any_spec = pl.BlockSpec(memory_space=pl.ANY)
    vmem_spec = pl.BlockSpec(memory_space=pltpu.VMEM)
    dma = pltpu.SemaphoreType.DMA
    return pl.pallas_call(
        functools.partial(exchange_kernel, n_row, n_col, part_dev),
        out_shape=(
            jax.ShapeDtypeStruct((rows_dev, PANEL), jnp.float32),
            jax.ShapeDtypeStruct((PANEL, cols_dev), jnp.float32),
            jax.ShapeDtypeStruct((PANEL, PANEL), jnp.float32),
            jax.ShapeDtypeStruct((TILE, PANEL), jnp.float32),
            jax.ShapeDtypeStruct((TILE, cols_dev), jnp.float32),
        ),
        in_specs=[any_spec, vmem_spec, vmem_spec],
        out_specs=(any_spec, vmem_spec, vmem_spec, vmem_spec, vmem_spec),
        scratch_shapes=[
            pltpu.VMEM((n_row, KS * part_dev // n_row, KS), jnp.float32),
            pltpu.VMEM(labels.shape, jnp.int32),
            pltpu.VMEM((n_row, KS * part_dev // n_row, cols_dev), jnp.bfloat16),
            pltpu.VMEM((n_row, KS * part_dev // n_row, cols_dev), jnp.bfloat16),
            pltpu.VMEM((n_col, TILE, cols_dev), jnp.float32),
            pltpu.VMEM((n_col, TILE, cols_dev), jnp.float32),
            dma((n_row,)),
            dma((n_row,)),
            dma((n_row,)),
            dma((n_row,)),
            dma((n_col,)),
            dma,
            dma((n_row,)),
            dma((2,)),
            dma((n_col,)),
            dma((n_col,)),
            dma((n_col,)),
            dma,
            dma((n_col,)),
            dma,
            dma((5,)),
        ],
        compiler_params=pltpu.CompilerParams(
            collective_id=0, has_side_effects=True, vmem_limit_bytes=VMEM_BYTES
        ),
    )(base, pieces, labels)


def full_dot(a, b, dims):
    return lax.dot_general(
        a, b, dims, precision=lax.Precision.HIGHEST, preferred_element_type=jnp.float32
    )


def split_dot(a, b, dims):
    a_high = a.astype(jnp.bfloat16)
    a_low = (a - a_high.astype(jnp.float32)).astype(jnp.bfloat16)
    b_high = b.astype(jnp.bfloat16)
    b_low = (b - b_high.astype(jnp.float32)).astype(jnp.bfloat16)
    dot = functools.partial(
        lax.dot_general, dimension_numbers=dims, preferred_element_type=jnp.float32
    )
    return dot(a_high, b_high) + (dot(a_high, b_low) + dot(a_low, b_high))


STEP = 4


def cholesky_and_inverse(work, block):
    row = lax.broadcasted_iota(jnp.int32, (TILE, TILE), 0)
    col = lax.broadcasted_iota(jnp.int32, (TILE, TILE), 1)
    groups = TILE // 8
    left = block.reshape(groups, 8, TILE)
    right = jnp.where(row == col, 1.0, 0.0).reshape(groups, 8, TILE)
    for k in range(0, TILE, STEP):
        g = k // 8
        s = k % 8
        lanes_left = [
            jnp.broadcast_to(left[0:1, s + i : s + i + 1, :], (1, 8, TILE)) for i in range(STEP)
        ]
        lanes_right = [
            jnp.broadcast_to(right[0:1, s + i : s + i + 1, :], (1, 8, TILE)) for i in range(STEP)
        ]
        cols = [
            jnp.broadcast_to(left[:, :, k + i : k + i + 1], left.shape) for i in range(STEP)
        ]
        heads = [
            [
                jnp.broadcast_to(cols[j][0:1, s + i : s + i + 1, :], (1, 8, TILE))
                for j in range(i + 1)
            ]
            for i in range(STEP)
        ]
        for i in range(STEP):
            scale = lax.rsqrt(heads[i][i])
            lanes_left[i] = lanes_left[i] * scale
            lanes_right[i] = lanes_right[i] * scale
            cols[i] = cols[i] * scale
            below = {}
            for m in range(i + 1, STEP):
                below[m] = heads[m][i] * scale
            for m in range(i + 1, STEP):
                for j in range(i + 1, m + 1):
                    heads[m][j] = heads[m][j] - below[m] * below[j]
                lanes_left[m] = lanes_left[m] - below[m] * lanes_left[i]
                lanes_right[m] = lanes_right[m] - below[m] * lanes_right[i]
                cols[m] = cols[m] - cols[i] * below[m]
        for i in range(STEP):
            work[k + i : k + i + 1, :TILE] = lanes_left[i][0, 0:1, :]
            work[k + i : k + i + 1, TILE:] = lanes_right[i][0, 0:1, :]
        if s + STEP == 8:
            left, right = left[1:], right[1:]
            cols = [x[1:] for x in cols]
        if left.shape[0]:
            for i in range(STEP):
                left = left - cols[i] * lanes_left[i]
                right = right - cols[i] * lanes_right[i]
    upper = jnp.where(row <= col, work[:, :TILE], 0.0)
    inverse = jnp.where(row >= col, work[:, TILE:], 0.0)
    return upper.T, inverse


def factor_kernel(
    base_ref, raw_ref, q_ref, diag_ref, top_ref, tile_ref, out_ref, work, inverse, panel, q_full
):
    r = lax.axis_index("row")
    c = lax.axis_index("col")
    rows_dev, cols_dev = base_ref.shape
    lower0, inverse0 = cholesky_and_inverse(work, diag_ref[:TILE, :TILE])
    lower10 = full_dot(diag_ref[TILE:, :TILE], inverse0, NT)
    lower1, inverse1 = cholesky_and_inverse(
        work, diag_ref[TILE:, TILE:] - full_dot(lower10, lower10, NT)
    )
    inverse[:TILE, :TILE] = inverse0
    inverse[:TILE, TILE:] = jnp.zeros((TILE, TILE), jnp.float32)
    inverse[TILE:, TILE:] = inverse1
    inverse[TILE:, :TILE] = -full_dot(inverse1, full_dot(lower10, inverse0, NN), NN)
    q_full[...] = full_dot(inverse[...], q_ref[...], NN)
    raw_ref[:TILE, :] = top_ref[...]

    def rows(i, carry):
        at = pl.ds(pl.multiple_of(i * TILE, TILE), TILE)
        panel[at, :] = split_dot(raw_ref[at, :], inverse[...], NT)
        return carry

    lax.fori_loop(0, rows_dev // TILE, rows, 0)

    @pl.when(r == 0)
    def _():
        panel[:TILE, :TILE] = lower0
        panel[:TILE, TILE:] = jnp.zeros((TILE, TILE), jnp.float32)

    @pl.when(r == 1)
    def _():
        panel[:TILE, :TILE] = lower10
        panel[:TILE, TILE:] = lower1

    def trailing(i, carry):
        at = pl.ds(pl.multiple_of(i * TILE, TILE), TILE)
        current = jnp.where(i == c, tile_ref[...], base_ref[at, :])
        out_ref[at, :] = current - split_dot(panel[at, :], q_full[...], NN)
        return carry

    lax.fori_loop(0, rows_dev // TILE, trailing, 0)

    @pl.when(r < 2)
    def _():
        out_ref[:TILE, :] = jnp.zeros((TILE, cols_dev), jnp.float32)

    @pl.when(c == 0)
    def _():
        out_ref[:, :PANEL] = panel[...]


def factorise(base, raw, q, diag, top, tile):
    rows_dev, cols_dev = base.shape
    vmem_spec = pl.BlockSpec(memory_space=pltpu.VMEM)
    return pl.pallas_call(
        factor_kernel,
        out_shape=jax.ShapeDtypeStruct(base.shape, jnp.float32),
        in_specs=[vmem_spec] * 6,
        out_specs=vmem_spec,
        scratch_shapes=[
            pltpu.VMEM((TILE, 2 * TILE), jnp.float32),
            pltpu.VMEM((PANEL, PANEL), jnp.float32),
            pltpu.VMEM((rows_dev, PANEL), jnp.float32),
            pltpu.VMEM((PANEL, cols_dev), jnp.float32),
        ],
        compiler_params=pltpu.CompilerParams(vmem_limit_bytes=VMEM_BYTES),
    )(base, raw, q, diag, top, tile)


def local(base_matrix, inverse_factors, coupling, positions, counts, owners):
    n_row = lax.axis_size("row")
    n_col = lax.axis_size("col")
    part_dev = coupling.shape[0]
    width = KS // n_row
    factor = jnp.einsum(
        "pbij,pbjk->pbik", inverse_factors, coupling, preferred_element_type=jnp.float32
    ).astype(jnp.bfloat16)
    schur_rows = jnp.einsum("pbik,pbil->pkl", factor, factor, preferred_element_type=jnp.float32)
    pieces = schur_rows.reshape(part_dev, n_row, width, KS).transpose(1, 0, 2, 3)
    pieces = pieces.reshape(n_row, part_dev * width, KS)
    within = jnp.arange(width, dtype=jnp.int32)
    group = jnp.arange(n_row, dtype=jnp.int32)
    usable = within[None, None, :] < counts[:, :, None]
    place = positions.reshape(part_dev, n_row, width)
    col_code = jnp.where(usable, group[None, :, None] * TILE + place, -1).reshape(part_dev, KS)
    row_code = jnp.where(usable, owners[:, None, None] * TILE + place, -1)
    row_code = row_code.transpose(1, 0, 2).reshape(n_row, 1, part_dev * width)
    labels = jnp.concatenate(
        [
            jnp.broadcast_to(col_code[None], (n_row, part_dev, KS)),
            jnp.pad(row_code, ((0, 0), (0, 0), (0, KS - part_dev * width))),
            jnp.zeros((n_row, 7 - part_dev, KS), jnp.int32),
        ],
        axis=1,
    )
    raw, q, diag, top, tile = exchange(n_row, n_col, base_matrix, pieces, labels)
    return factorise(base_matrix, raw, q, diag, top, tile)


def solution(mesh):
    in_specs = (
        P("row", "col"),
        P(("row", "col"), None, None, None),
        P(("row", "col"), None, None, None),
        P(("row", "col"), None),
        P(("row", "col"), None),
        P(("row", "col")),
    )
    out_specs = P("row", "col")
    return jax.shard_map(local, mesh=mesh, in_specs=in_specs, out_specs=out_specs, check_vma=False)
```

time: 392 us -> 123 us (0.31)
  waiting for transfers between devices: 220 us -> 0 us
  Pallas kernels: 0 us -> 112 us
  other arithmetic: 52.6 us -> 1.65 us
  blocking collectives: 27.9 us -> 0 us
  matrix products: 33.2 us -> 6.38 us
  starting transfers between devices: 20.3 us -> 0 us
  local copies, waits for them, and re-layouts: 23 us -> 2.86 us
  between operations: 13.4 us -> 0.04 us
    psum x4 -> x0, waiting for transfers between devices: 173 us -> none  [spread(): return lax.psum(jnp.where(mine, value, jnp.zeros_like(value)), axis)]
    pallas_call x0 -> x2, Pallas kernels: none -> 112 us  [the longest x1 91.4 us: exchange(): pl.pallas_call(functools.partial(exchange_kernel, n_row, n_col, part_dev)...]
    all_to_all x4 -> x0, waiting for transfers between devices: 47.3 us -> none  [the longest x1 24 us: local(): lax.all_to_all(pieces, 'row', split_axis=1, concat_axis=1, tiled=True)]
    another operation x10 -> x0, other arithmetic: 46 us -> none  [the longest x6 24.9 us: panel(): lower = jnp.linalg.cholesky(diagonal)]
    all_gather x2 -> x0, blocking collectives: 27.9 us -> none  [panel(): cols_part = lax.all_gather(own_tile, 'row', axis=0, tiled=True)]
    dot_general x8 -> x0, matrix products: 26.2 us -> none  [the longest x1 5.41 us: local(): jnp.einsum('isr,isc->rc', row_onehot, spread_cols, precision=lax.Precisio...]
    all_to_all x4 -> x0, starting transfers between devices: 19.5 us -> none  [the longest x1 6.32 us: local(): lax.all_to_all(labels, 'row', split_axis=1, concat_axis=1, tiled=True)]
    reshape x5 -> x3, local copies, waits for them, and re-layouts: 7.73 us -> 0.93 us  [the longest x1 0.77 us: local(): place = positions.reshape(part_dev, n_row, width)]
  transfers between devices with their start and end apart: 8 -> 0, of which waited for: 6 -> 0; matrix products, arithmetic and copies ran while one was open for 5% -> 0% of each run, Pallas kernels for 0% -> 0%
where the time goes in v1:
time: 123 us; the launch traced here: 122 us
  Pallas kernels  112 us (91%)
  matrix products  6.38 us (5%)
  local copies, waits for them, and re-layouts  2.86 us (2%)
  other arithmetic  1.65 us (1%)
    pallas_call x1, Pallas kernels, exchange(): pl.pallas_call(functools.partial(exchange_kernel, n_row, n_col, part_dev)...  91.4 us
    pallas_call x1, Pallas kernels, factorise(): pl.pallas_call(factor_kernel, out_shape=jax.ShapeDtypeStruct(base.shape,...  20.2 us
    dot_general x1, matrix products, local(): jnp.einsum('pbik,pbil->pkl', factor, factor, preferred_element_type=jnp.f...  6.38 us

profile of v1, /device:TPU:0, one launch (start us, length us, event | category | flops | bytes accessed | tf_op | source)
XLA Modules:
  0.0 122.5 jit_solution(6308069982808209856)
XLA Ops:
  0.0 0.0 copy-start
  0.0 0.8 broadcast_multiply_fusion
  0.8 0.1 pad.2.clone
  0.9 0.1 add.22
  1.0 0.1 add.23
  1.1 0.8 copy.9
  1.8 0.1 lt.26
  1.9 0.8 reshape.33
  2.7 0.1 fusion.5
  2.8 0.1 reshape.34
  2.8 0.8 lt.28.clone
  3.6 0.1 lt.29
  3.7 0.7 add_select_fusion
  4.4 0.1 add_add_fusion.labels_ref
  4.5 0.0 copy-done
  4.5 6.4 %fusion = f32[4,256,256,1]{2,1,3,0:T(8,128)S(1)} fusion(bf16[4,2,512,512]{3,2,1,0:T(8,128)(2,1)} %param.7, bf16[4,2,512,256]{3,2,1,0:T(8,128)(2,1)S(1)} %copy-done), kind=kOutput, calls=%fused_computation | convolution fusion | flops 1611661312 | bytes 7340032 | tf_op jit(solution)/shard_map/pbik,pbil->pkl/dot_general | solution.py:489
  10.8 0.1 copy.8
  10.9 91.4 %shard_map.64 = (f32[1024,256]{1,0:T(8,128)S(1)}, f32[256,512]{1,0:T(8,128)S(1)}, f32[256,256]{1,0:T(8,128)S(1)}, f32[128,256]{1,0:T(8,128)S(1)}, f32[128,512]{1,0:T(8,128)S(1)}) custom-call(f32[1024,512]{1,0:T(8,128)} %base_ref.3, f32[4,256,256]{2,1,0:T(8,128)S(1)} %bitcast.11, s32[4,8,256]{2,1,0:T(8,128)S(1)} %add_add_fusion.labels_ref), custom_call_target="tpu_custom_call" | custom-call | tf_op jit(solution)/shard_map/pallas_call | solution.py:297
  102.3 20.2 %shard_map.65 = f32[1024,512]{1,0:T(8,128)} custom-call(f32[1024,512]{1,0:T(8,128)} %base_ref.3, f32[1024,256]{1,0:T(8,128)S(1)} %get-tuple-element.10.raw_ref, f32[256,512]{1,0:T(8,128)S(1)} %get-tuple-element.11.q_ref, f32[256,256]{1,0:T(8,128)S(1)} %get-tuple-element.12.diag_ref, f32[128,256]{1,0:T(8,128)S(1)} %get-tuple-element.13.top_ref, ...), custom_call_target="tpu_custom_call" | custom-call | tf_op jit(solution)/shard_map/pallas_call | solution.py:466
  (4 shorter events, 0.0 us)
Async XLA Ops:
  0.0 4.5 %copy-start = (bf16[4,2,512,256]{3,2,1,0:T(8,128)(2,1)S(1)}, bf16[4,2,512,256]{3,2,1,0:T(8,128)(2,1)}, u32[]{:S(2)}) copy-start(bf16[4,2,512,256]{3,2,1,0:T(8,128)(2,1)} %param.8) | copy-start | bytes 6291460

commit v2 on v1

--- a/solution.py
+++ b/solution.py
@@ -33,6 +33,7 @@
     wide_hi,
     wide_lo,
     partial,
+    paired,
     landed,
     piece_send,
     piece_recv,
@@ -42,30 +43,111 @@
     raw_recv,
     q_send,
     q_recv,
+    pair_send,
+    pair_recv,
     part_send,
     part_recv,
+    deal_send,
+    top_send,
+    top_recv,
+    lift_send,
+    lift_recv,
     diag_send,
     diag_recv,
-    top_send,
-    top_recv,
     local_sem,
 ):
     r = lax.axis_index("row")
     c = lax.axis_index("col")
     width = KS // n_row
     cols_dev = n_row * TILE
+    chunk = TILE // n_col
+    parity = lax.rem(c, 2)
+    twin = c + 1 - 2 * parity
+    pairs = n_col // 2
+    place = lax.div(c, 2)
 
     def row_peer(d):
         return lax.rem(r + d, n_row)
 
-    def row_source(d):
-        return lax.rem(r + n_row - d, n_row)
-
     def col_peer(d):
         return lax.rem(c + d, n_col)
 
-    def col_source(d):
-        return lax.rem(c + n_col - d, n_col)
+    def send(src, dst, send_sem, recv_sem, axis, to):
+        return pltpu.make_async_remote_copy(
+            src_ref=src,
+            dst_ref=dst,
+            send_sem=send_sem,
+            recv_sem=recv_sem,
+            device_id={axis: to},
+            device_id_type=MESH,
+        )
+
+    def piece_copy(to, slot):
+        return send(
+            pieces_ref.at[to], got.at[slot], piece_send.at[to], piece_recv.at[slot], "row", to
+        )
+
+    def label_copy(to, slot):
+        return send(
+            labels_ref.at[to], got_labels.at[slot], label_send.at[to], label_recv.at[slot], "row", to
+        )
+
+    def raw_deal(to):
+        at = pl.ds(to * TILE, TILE)
+        return send(
+            base_ref.at[at, pl.ds(0, PANEL)],
+            raw_ref.at[at],
+            raw_send.at[to],
+            raw_recv.at[to],
+            "col",
+            to,
+        )
+
+    def raw_copy(to, index):
+        at = pl.ds(index * TILE, TILE)
+        return send(
+            raw_ref.at[at], raw_ref.at[at], raw_send.at[to], raw_recv.at[index], "col", to
+        )
+
+    def q_copy(to, half):
+        at = pl.ds(half * TILE, TILE)
+        return send(q_ref.at[at], q_ref.at[at], q_send.at[to], q_recv.at[half], "row", to)
+
+    def q_rest_copy(to, half):
+        at = q_ref.at[pl.ds(half * TILE, TILE), pl.ds(PANEL, cols_dev - PANEL)]
+        return send(at, at, q_send.at[to], q_recv.at[half], "row", to)
+
+    def pair_copy(j):
+        owner = 2 * j + 1 - parity
+        return send(partial.at[owner], paired.at[j], pair_send.at[j], pair_recv.at[j], "col", twin)
+
+    def part_copy(j, slot):
+        owner = 2 * j + parity
+        return send(
+            partial.at[owner], landed.at[slot], part_send.at[j], part_recv.at[slot], "col", owner
+        )
+
+    def deal_copy(to):
+        at = top_ref.at[pl.ds(to * chunk, chunk)]
+        return send(at, at, deal_send.at[to], top_recv.at[to], "col", to)
+
+    def top_copy(to, index):
+        at = top_ref.at[pl.ds(index * chunk, chunk)]
+        return send(at, at, top_send.at[to], top_recv.at[index], "col", to)
+
+    def lift_copy(to, half):
+        return send(
+            top_ref.at[pl.ds(c * chunk, chunk)],
+            diag_ref.at[pl.ds(half * TILE + c * chunk, chunk)],
+            lift_send.at[to],
+            lift_recv.at[half],
+            "row",
+            to,
+        )
+
+    def diag_copy(to, half, index):
+        at = diag_ref.at[pl.ds(half * TILE + index * chunk, chunk)]
+        return send(at, at, diag_send.at[half, to], diag_recv.at[half, index], "col", to)
 
     barrier = pltpu.get_barrier_semaphore()
     for d in range(1, n_row):
@@ -73,76 +155,6 @@
     for d in range(1, n_col):
         pl.semaphore_signal(barrier, inc=1, device_id={"col": col_peer(d)}, device_id_type=MESH)
     pl.semaphore_wait(barrier, n_row + n_col - 2)
-
-    def piece_copy(to, slot):
-        return pltpu.make_async_remote_copy(
-            src_ref=pieces_ref.at[to],
-            dst_ref=got.at[slot],
-            send_sem=piece_send.at[to],
-            recv_sem=piece_recv.at[slot],
-            device_id={"row": to},
-            device_id_type=MESH,
-        )
-
-    def label_copy(to, slot):
-        return pltpu.make_async_remote_copy(
-            src_ref=labels_ref.at[to],
-            dst_ref=got_labels.at[slot],
-            send_sem=label_send.at[to],
-            recv_sem=label_recv.at[slot],
-            device_id={"row": to},
-            device_id_type=MESH,
-        )
-
-    def raw_copy(to):
-        return pltpu.make_async_remote_copy(
-            src_ref=base_ref.at[:, pl.ds(0, PANEL)],
-            dst_ref=raw_ref,
-            send_sem=raw_send.at[to],
-            recv_sem=raw_recv,
-            device_id={"col": to},
-            device_id_type=MESH,
-        )
-
-    def q_copy(to, half):
-        return pltpu.make_async_remote_copy(
-            src_ref=q_ref.at[pl.ds(half * TILE, TILE)],
-            dst_ref=q_ref.at[pl.ds(half * TILE, TILE)],
-            send_sem=q_send.at[to],
-            recv_sem=q_recv.at[half],
-            device_id={"row": to},
-            device_id_type=MESH,
-        )
-
-    def part_copy(to, slot):
-        return pltpu.make_async_remote_copy(
-            src_ref=partial.at[to],
-            dst_ref=landed.at[slot],
-            send_sem=part_send.at[to],
-            recv_sem=part_recv.at[slot],
-            device_id={"col": to},
-            device_id_type=MESH,
-        )
-
-    def diag_copy(to):
-        return pltpu.make_async_remote_copy(
-            src_ref=diag_ref,
-            dst_ref=diag_ref,
-            send_sem=diag_send.at[to],
-            recv_sem=diag_recv,
-            device_id={"col": to},
-            device_id_type=MESH,
-        )
-
-    def top_copy(to):
-        return pltpu.make_async_remote_copy(
-            src_ref=top_ref,
-            dst_ref=top_ref,
-            send_sem=top_send.at[to],
-            recv_sem=top_recv,
-            device_id={"col": to},
-            device_id_type=MESH,
-        )
 
     for d in range(1, n_row):
         label_copy(row_peer(d), r).start()
@@ -152,21 +164,20 @@
     own_label = pltpu.make_async_copy(labels_ref.at[r], got_labels.at[r], local_sem.at[1])
     own_piece.start()
     own_label.start()
-
-    @pl.when(c == 0)
-    def _():
-        for to in range(1, n_col):
-            raw_copy(to).start()
-        own_raw = pltpu.make_async_copy(
-            base_ref.at[:, pl.ds(0, PANEL)], raw_ref, local_sem.at[2]
-        )
-        own_raw.start()
-        own_raw.wait()
-
     own_tile = pltpu.make_async_copy(
         base_ref.at[pl.ds(c * TILE, TILE)], tile_ref, local_sem.at[3]
     )
     own_tile.start()
+
+    @pl.when(c == 0)
+    def _():
+        for to in range(1, n_col):
+            raw_deal(to).start()
+        own_raw = pltpu.make_async_copy(
+            base_ref.at[:, pl.ds(0, PANEL)], raw_ref, local_sem.at[2]
+        )
+        own_raw.start()
+        own_raw.wait()
 
     own_piece.wait()
     own_label.wait()
@@ -187,6 +198,16 @@
 
     widen(r)
 
+    @pl.when(c != 0)
+    def _():
+        raw_copy(0, c).wait_recv()
+        for d in range(1, n_col):
+            to = col_peer(d)
+
+            @pl.when(to != 0)
+            def _():
+                raw_copy(to, c).start()
+
     def arrive(d, carry):
         src = lax.rem(r + n_row - d, n_row)
         label_copy(row_peer(1), src).wait_recv()
@@ -196,10 +217,6 @@
 
     lax.fori_loop(1, n_row, arrive, 0)
 
-    def send_q(half):
-        for d in range(1, n_row):
-            q_copy(row_peer(d), half).start()
-
     for half in range(2):
 
         @pl.when((r == half) & (c != 0))
@@ -209,9 +226,10 @@
             )
             own_q.start()
             own_q.wait()
-            send_q(half)
-
-    def gather_owner(o, carry):
+            for d in range(1, n_row):
+                q_copy(row_peer(d), half).start()
+
+    def gather_owner(o):
         total = jnp.zeros((TILE, cols_dev), jnp.float32)
         for src in range(n_row):
             code = got_labels[src, pl.ds(part_dev, 1), :][:, : part_dev * width]
@@ -221,71 +239,160 @@
             total += lax.dot_general(onehot, wide_lo[src], NN, preferred_element_type=jnp.float32)
         partial[o] = total
 
-        @pl.when(o != c)
-        def _():
-            part_copy(o, c).start()
-
+    def gather_pair(j, carry):
+        gather_owner(2 * j + 1 - parity)
+        pair_copy(j).start()
         return carry
 
-    lax.fori_loop(0, n_col, gather_owner, 0)
+    lax.fori_loop(0, pairs, gather_pair, 0)
+
+    def gather_own(j, carry):
+        owner = 2 * j + parity
+        gather_owner(owner)
+        pair_copy(j).wait_recv()
+        partial[owner] = partial[owner] + paired[j]
+
+        @pl.when(owner != c)
+        def _():
+            part_copy(j, place).start()
+
+        return carry
+
+    lax.fori_loop(0, pairs, gather_own, 0)
 
     own_tile.wait()
-    summed = partial[c]
-    for d in range(1, n_col):
-        src = col_source(d)
-        part_copy(col_peer(1), src).wait_recv()
-        summed += landed[src]
-    tile_ref[...] = tile_ref[...] - summed
+    tile_ref[...] = tile_ref[...] - partial[c]
+
+    def collect(d, carry):
+        slot = lax.rem(place + pairs - d, pairs)
+        part_copy(lax.rem(place + 1, pairs), slot).wait_recv()
+        tile_ref[...] = tile_ref[...] - landed[slot]
+        return carry
+
+    lax.fori_loop(1, pairs, collect, 0)
+
+    @pl.when(c == 0)
+    def _():
+        top_ref[...] = tile_ref[:, :PANEL]
+        for to in range(1, n_col):
+            deal_copy(to).start()
+
+    @pl.when(c != 0)
+    def _():
+        deal_copy(c).wait_recv()
 
     for half in range(2):
 
+        @pl.when(r == half)
+        def _():
+            for d in range(1, n_row):
+                lift_copy(row_peer(d), half).start()
+
+    def top_sends(act):
+        for d in range(1, n_col):
+            to = col_peer(d)
+
+            @pl.when(to != 0)
+            def _():
+                act(top_copy(to, c))
+
+    top_sends(lambda copy: copy.start())
+
+    for half in range(2):
+
+        @pl.when(r != half)
+        def _():
+            lift_copy(row_peer(1), half).wait_recv()
+            for d in range(1, n_col):
+                diag_copy(col_peer(d), half, c).start()
+
+    for half in range(2):
+
         @pl.when((r == half) & (c == 0))
         def _():
             q_ref[pl.ds(half * TILE, TILE), :] = tile_ref[...]
-            send_q(half)
-
-    @pl.when(c == 0)
-    def _():
-        top_ref[...] = tile_ref[:, :PANEL]
+            for d in range(1, n_row):
+                q_rest_copy(row_peer(d), half).start()
+
+    @pl.when(c != 0)
+    def _():
+        for d in range(1, n_col):
+            index = col_peer(d)
+            top_copy(index, index).wait_recv()
+
+            @pl.when(index != 0)
+            def _():
+                raw_copy(index, index).wait_recv()
 
     for half in range(2):
 
+        @pl.when(r == half)
+        def _():
+            diag_ref[pl.ds(half * TILE, TILE), :] = top_ref[...]
+
         @pl.when(r != half)
         def _():
+            for d in range(1, n_col):
+                index = col_peer(d)
+                diag_copy(index, half, index).wait_recv()
+
+        @pl.when((r != half) & (c != 0))
+        def _():
             q_copy(row_peer(1), half).wait_recv()
 
-    @pl.when(c == 0)
-    def _():
-        diag_ref[...] = q_ref[:, :PANEL]
-        for to in range(1, n_col):
-            diag_copy(to).start()
-        for to in range(1, n_col):
-            top_copy(to).start()
-
-    @pl.when(c != 0)
-    def _():
-        diag_copy(0).wait_recv()
-        top_copy(0).wait_recv()
-        raw_copy(0).wait_recv()
-
-    @pl.when(c == 0)
-    def _():
-        for to in range(1, n_col):
-            diag_copy(to).wait_send()
-            top_copy(to).wait_send()
-            raw_copy(to).wait_send()
+        @pl.when((r != half) & (c == 0))
+        def _():
+            q_rest_copy(row_peer(1), half).wait_recv()
+            q_ref[pl.ds(half * TILE, TILE), :PANEL] = diag_ref[pl.ds(half * TILE, TILE), :]
 
     for d in range(1, n_row):
         label_copy(row_peer(d), r).wait_send()
         piece_copy(row_peer(d), r).wait_send()
-    for d in range(1, n_col):
-        part_copy(col_peer(d), c).wait_send()
+
+    @pl.when(c == 0)
+    def _():
+        for to in range(1, n_col):
+            raw_deal(to).wait_send()
+            deal_copy(to).wait_send()
+
+    @pl.when(c != 0)
+    def _():
+        for d in range(1, n_col):
+            to = col_peer(d)
+
+            @pl.when(to != 0)
+            def _():
+                raw_copy(to, c).wait_send()
+
+    for j in range(pairs):
+        pair_copy(j).wait_send()
+
+        @pl.when(j != place)
+        def _():
+            part_copy(j, place).wait_send()
+
+    top_sends(lambda copy: copy.wait_send())
     for half in range(2):
 
         @pl.when(r == half)
+        def _():
+            for d in range(1, n_row):
+                lift_copy(row_peer(d), half).wait_send()
+
+        @pl.when(r != half)
+        def _():
+            for d in range(1, n_col):
+                diag_copy(col_peer(d), half, c).wait_send()
+
+        @pl.when((r == half) & (c != 0))
         def _():
             for d in range(1, n_row):
                 q_copy(row_peer(d), half).wait_send()
+
+        @pl.when((r == half) & (c == 0))
+        def _():
+            for d in range(1, n_row):
+                q_rest_copy(row_peer(d), half).wait_send()
 
 
 def exchange(n_row, n_col, base, pieces, labels):
@@ -311,21 +418,27 @@
             pltpu.VMEM((n_row, KS * part_dev // n_row, cols_dev), jnp.bfloat16),
             pltpu.VMEM((n_row, KS * part_dev // n_row, cols_dev), jnp.bfloat16),
             pltpu.VMEM((n_col, TILE, cols_dev), jnp.float32),
-            pltpu.VMEM((n_col, TILE, cols_dev), jnp.float32),
+            pltpu.VMEM((n_col // 2, TILE, cols_dev), jnp.float32),
+            pltpu.VMEM((n_col // 2, TILE, cols_dev), jnp.float32),
             dma((n_row,)),
             dma((n_row,)),
             dma((n_row,)),
             dma((n_row,)),
             dma((n_col,)),
-            dma,
+            dma((n_col,)),
             dma((n_row,)),
             dma((2,)),
+            dma((n_col // 2,)),
+            dma((n_col // 2,)),
+            dma((n_col // 2,)),
+            dma((n_col // 2,)),
             dma((n_col,)),
             dma((n_col,)),
             dma((n_col,)),
-            dma,
-            dma((n_col,)),
-            dma,
+            dma((n_row,)),
+            dma((2,)),
+            dma((2, n_col)),
+            dma((2, n_col)),
             dma((5,)),
         ],
         compiler_params=pltpu.CompilerParams(

time: 123 us -> 89.6 us (0.73)
  Pallas kernels: 112 us -> 77.5 us
    pallas_call x1, Pallas kernels: 91.4 us -> 57.4 us  [exchange(): pl.pallas_call(functools.partial(exchange_kernel, n_row, n_col, part_dev)...]
where the time goes in v2:
time: 89.6 us; the launch traced here: 88.5 us
  Pallas kernels  77.5 us (86%)
  matrix products  6.38 us (7%)
  local copies, waits for them, and re-layouts  2.86 us (3%)
  other arithmetic  1.65 us (2%)
    pallas_call x1, Pallas kernels, exchange(): pl.pallas_call(functools.partial(exchange_kernel, n_row, n_col, part_dev)...  57.4 us
    pallas_call x1, Pallas kernels, factorise(): pl.pallas_call(factor_kernel, out_shape=jax.ShapeDtypeStruct(base.shape,...  20.2 us
    dot_general x1, matrix products, local(): jnp.einsum('pbik,pbil->pkl', factor, factor, preferred_element_type=jnp.f...  6.38 us

profile of v2, /device:TPU:0, one launch (start us, length us, event | category | flops | bytes accessed | tf_op | source)
XLA Modules:
  0.0 88.5 jit_solution(5643240569967884685)
XLA Ops:
  0.0 0.0 copy-start
  0.0 0.8 broadcast_multiply_fusion
  0.8 0.1 pad.2.clone
  0.9 0.1 add.22
  1.0 0.1 add.23
  1.1 0.8 copy.9
  1.8 0.1 lt.26
  1.9 0.8 reshape.33
  2.7 0.1 fusion.5
  2.8 0.1 reshape.34
  2.8 0.8 lt.28.clone
  3.6 0.1 lt.29
  3.7 0.7 add_select_fusion
  4.4 0.1 add_add_fusion.labels_ref
  4.5 0.0 copy-done
  4.5 6.4 %fusion = f32[4,256,256,1]{2,1,3,0:T(8,128)S(1)} fusion(bf16[4,2,512,512]{3,2,1,0:T(8,128)(2,1)} %param.7, bf16[4,2,512,256]{3,2,1,0:T(8,128)(2,1)S(1)} %copy-done), kind=kOutput, calls=%fused_computation | convolution fusion | flops 1611661312 | bytes 7340032 | tf_op jit(solution)/shard_map/pbik,pbil->pkl/dot_general | solution.py:602
  10.8 0.1 copy.8
  10.9 57.4 %shard_map.64 = (f32[1024,256]{1,0:T(8,128)S(1)}, f32[256,512]{1,0:T(8,128)S(1)}, f32[256,256]{1,0:T(8,128)S(1)}, f32[128,256]{1,0:T(8,128)S(1)}, f32[128,512]{1,0:T(8,128)S(1)}) custom-call(f32[1024,512]{1,0:T(8,128)} %base_ref.3, f32[4,256,256]{2,1,0:T(8,128)S(1)} %bitcast.11, s32[4,8,256]{2,1,0:T(8,128)S(1)} %add_add_fusion.labels_ref), custom_call_target="tpu_custom_call" | custom-call | tf_op jit(solution)/shard_map/pallas_call | solution.py:404
  68.3 20.2 %shard_map.65 = f32[1024,512]{1,0:T(8,128)} custom-call(f32[1024,512]{1,0:T(8,128)} %base_ref.3, f32[1024,256]{1,0:T(8,128)S(1)} %get-tuple-element.10.raw_ref, f32[256,512]{1,0:T(8,128)S(1)} %get-tuple-element.11.q_ref, f32[256,256]{1,0:T(8,128)S(1)} %get-tuple-element.12.diag_ref, f32[128,256]{1,0:T(8,128)S(1)} %get-tuple-element.13.top_ref, ...), custom_call_target="tpu_custom_call" | custom-call | tf_op jit(solution)/shard_map/pallas_call | solution.py:579
  (4 shorter events, 0.0 us)
Async XLA Ops:
  0.0 4.5 %copy-start = (bf16[4,2,512,256]{3,2,1,0:T(8,128)(2,1)S(1)}, bf16[4,2,512,256]{3,2,1,0:T(8,128)(2,1)}, u32[]{:S(2)}) copy-start(bf16[4,2,512,256]{3,2,1,0:T(8,128)(2,1)} %param.8) | copy-start | bytes 6291460

commit v3 on v2

--- a/solution.py
+++ b/solution.py
@@ -14,6 +14,7 @@
 MESH = pl.DeviceIdType.MESH
 NT = (((1,), (1,)), ((), ()))
 NN = (((1,), (0,)), ((), ()))
+TN = (((0,), (0,)), ((), ()))
 
 
 def exchange_kernel(
@@ -21,13 +22,20 @@
     n_col,
     part_dev,
     base_ref,
-    pieces_ref,
-    labels_ref,
+    factors_ref,
+    coupling_ref,
+    positions_ref,
+    counts_ref,
+    owners_ref,
     raw_ref,
     q_ref,
     diag_ref,
     top_ref,
     tile_ref,
+    factors,
+    couplings,
+    pieces,
+    labels,
     got,
     got_labels,
     wide_hi,
@@ -55,6 +63,7 @@
     diag_send,
     diag_recv,
     local_sem,
+    load_sem,
 ):
     r = lax.axis_index("row")
     c = lax.axis_index("col")
@@ -82,14 +91,15 @@
             device_id_type=MESH,
         )
 
-    def piece_copy(to, slot):
+    def piece_copy(to, slot, p):
+        at = pl.ds(p * width, width)
         return send(
-            pieces_ref.at[to], got.at[slot], piece_send.at[to], piece_recv.at[slot], "row", to
+            pieces.at[to, at], got.at[slot, at], piece_send.at[to, p], piece_recv.at[slot, p], "row", to
         )
 
     def label_copy(to, slot):
         return send(
-            labels_ref.at[to], got_labels.at[slot], label_send.at[to], label_recv.at[slot], "row", to
+            labels.at[to], got_labels.at[slot], label_send.at[to], label_recv.at[slot], "row", to
         )
 
     def raw_deal(to):
@@ -111,11 +121,11 @@
 
     def q_copy(to, half):
         at = pl.ds(half * TILE, TILE)
-        return send(q_ref.at[at], q_ref.at[at], q_send.at[to], q_recv.at[half], "row", to)
+        return send(q_ref.at[at], q_ref.at[at], q_send.at[half, to], q_recv.at[half], "row", to)
 
     def q_rest_copy(to, half):
         at = q_ref.at[pl.ds(half * TILE, TILE), pl.ds(PANEL, cols_dev - PANEL)]
-        return send(at, at, q_send.at[to], q_recv.at[half], "row", to)
+        return send(at, at, q_send.at[half, to], q_recv.at[half], "row", to)
 
     def pair_copy(j):
         owner = 2 * j + 1 - parity
@@ -149,20 +159,45 @@
         at = diag_ref.at[pl.ds(half * TILE + index * chunk, chunk)]
         return send(at, at, diag_send.at[half, to], diag_recv.at[half, index], "col", to)
 
+    def load(p, part):
+        src, dst = ((factors_ref, factors), (coupling_ref, couplings))[part]
+        return pltpu.make_async_copy(src.at[p], dst.at[p], load_sem.at[part, p])
+
+    for p in range(part_dev):
+        load(p, 0).start()
+        load(p, 1).start()
+
     barrier = pltpu.get_barrier_semaphore()
     for d in range(1, n_row):
         pl.semaphore_signal(barrier, inc=1, device_id={"row": row_peer(d)}, device_id_type=MESH)
     for d in range(1, n_col):
         pl.semaphore_signal(barrier, inc=1, device_id={"col": col_peer(d)}, device_id_type=MESH)
+
+    lane = lax.broadcasted_iota(jnp.int32, (1, KS), 1)
+    places = positions_ref[...]
+    usable, columns = [], []
+    for p in range(part_dev):
+        limit = jnp.zeros((1, KS), jnp.int32)
+        offset = jnp.zeros((1, KS), jnp.int32)
+        for g in range(n_row):
+            inside = (lane >= g * width) & (lane < (g + 1) * width)
+            limit = jnp.where(inside, counts_ref[p, g] + g * width, limit)
+            offset = jnp.where(inside, g * TILE, offset)
+        used = lane < limit
+        columns.append(jnp.where(used, places[p : p + 1, :] + offset, -1))
+        usable.append(jnp.where(used, places[p : p + 1, :] + owners_ref[p] * TILE, -1))
+    column_codes = jnp.concatenate(columns, axis=0)
+    for g in range(n_row):
+        labels[g, :part_dev, :] = column_codes
+        labels[g, part_dev : part_dev + 1, : part_dev * width] = jnp.concatenate(
+            [x[:, g * width : (g + 1) * width] for x in usable], axis=1
+        )
+
     pl.semaphore_wait(barrier, n_row + n_col - 2)
 
     for d in range(1, n_row):
         label_copy(row_peer(d), r).start()
-    for d in range(1, n_row):
-        piece_copy(row_peer(d), r).start()
-    own_piece = pltpu.make_async_copy(pieces_ref.at[r], got.at[r], local_sem.at[0])
-    own_label = pltpu.make_async_copy(labels_ref.at[r], got_labels.at[r], local_sem.at[1])
-    own_piece.start()
+    own_label = pltpu.make_async_copy(labels.at[r], got_labels.at[r], local_sem.at[1])
     own_label.start()
     own_tile = pltpu.make_async_copy(
         base_ref.at[pl.ds(c * TILE, TILE)], tile_ref, local_sem.at[3]
@@ -179,6 +214,22 @@
         own_raw.start()
         own_raw.wait()
 
+    for p in range(part_dev):
+        load(p, 0).wait()
+        load(p, 1).wait()
+        schur = jnp.zeros((KS, KS), jnp.float32)
+        for b in range(factors_ref.shape[1]):
+            factor = jnp.dot(
+                factors[p, b], couplings[p, b], preferred_element_type=jnp.float32
+            ).astype(jnp.bfloat16)
+            schur += lax.dot_general(factor, factor, TN, preferred_element_type=jnp.float32)
+        for g in range(n_row):
+            pieces[g, pl.ds(p * width, width), :] = schur[g * width : (g + 1) * width, :]
+        for d in range(1, n_row):
+            piece_copy(row_peer(d), r, p).start()
+
+    own_piece = pltpu.make_async_copy(pieces.at[r], got.at[r], local_sem.at[0])
+    own_piece.start()
     own_piece.wait()
     own_label.wait()
 
@@ -211,11 +262,23 @@
     def arrive(d, carry):
         src = lax.rem(r + n_row - d, n_row)
         label_copy(row_peer(1), src).wait_recv()
-        piece_copy(row_peer(1), src).wait_recv()
+        for p in range(part_dev):
+            piece_copy(row_peer(1), src, p).wait_recv()
         widen(src)
         return carry
 
     lax.fori_loop(1, n_row, arrive, 0)
+
+    def q_out(make, half, act):
+        if half > 0:
+            act(make(half - 1, half))
+        act(make(half + 1, half))
+
+    def q_forward(make, half, first, last):
+        @pl.when((r > half) & (r >= first) & (r < last))
+        def _():
+            make(r + 1, half).wait_recv()
+            make(r + 1, half).start()
 
     for half in range(2):
 
@@ -226,8 +289,7 @@
             )
             own_q.start()
             own_q.wait()
-            for d in range(1, n_row):
-                q_copy(row_peer(d), half).start()
+            q_out(q_copy, half, lambda copy: copy.start())
 
     def gather_owner(o):
         total = jnp.zeros((TILE, cols_dev), jnp.float32)
@@ -246,6 +308,11 @@
 
     lax.fori_loop(0, pairs, gather_pair, 0)
 
+    @pl.when(c != 0)
+    def _():
+        for half in range(2):
+            q_forward(q_copy, half, 0, 2)
+
     def gather_own(j, carry):
         owner = 2 * j + parity
         gather_owner(owner)
@@ -311,8 +378,17 @@
         @pl.when((r == half) & (c == 0))
         def _():
             q_ref[pl.ds(half * TILE, TILE), :] = tile_ref[...]
-            for d in range(1, n_row):
-                q_rest_copy(row_peer(d), half).start()
+            q_out(q_rest_copy, half, lambda copy: copy.start())
+
+    for half in range(2):
+
+        @pl.when(c != 0)
+        def _():
+            q_forward(q_copy, half, 2, n_row - 1)
+
+        @pl.when(c == 0)
+        def _():
+            q_forward(q_rest_copy, half, 0, n_row - 1)
 
     @pl.when(c != 0)
     def _():
@@ -336,18 +412,22 @@
                 index = col_peer(d)
                 diag_copy(index, half, index).wait_recv()
 
-        @pl.when((r != half) & (c != 0))
+        @pl.when(((r < half) | (r == n_row - 1)) & (c != 0))
         def _():
             q_copy(row_peer(1), half).wait_recv()
 
+        @pl.when(((r < half) | (r == n_row - 1)) & (c == 0))
+        def _():
+            q_rest_copy(row_peer(1), half).wait_recv()
+
         @pl.when((r != half) & (c == 0))
         def _():
-            q_rest_copy(row_peer(1), half).wait_recv()
             q_ref[pl.ds(half * TILE, TILE), :PANEL] = diag_ref[pl.ds(half * TILE, TILE), :]
 
     for d in range(1, n_row):
         label_copy(row_peer(d), r).wait_send()
-        piece_copy(row_peer(d), r).wait_send()
+        for p in range(part_dev):
+            piece_copy(row_peer(d), r, p).wait_send()
 
     @pl.when(c == 0)
     def _():
@@ -386,18 +466,25 @@
 
         @pl.when((r == half) & (c != 0))
         def _():
-            for d in range(1, n_row):
-                q_copy(row_peer(d), half).wait_send()
+            q_out(q_copy, half, lambda copy: copy.wait_send())
+
+        @pl.when((r > half) & (r < n_row - 1) & (c != 0))
+        def _():
+            q_copy(r + 1, half).wait_send()
 
         @pl.when((r == half) & (c == 0))
         def _():
-            for d in range(1, n_row):
-                q_rest_copy(row_peer(d), half).wait_send()
-
-
-def exchange(n_row, n_col, base, pieces, labels):
+            q_out(q_rest_copy, half, lambda copy: copy.wait_send())
+
+        @pl.when((r > half) & (r < n_row - 1) & (c == 0))
+        def _():
+            q_rest_copy(r + 1, half).wait_send()
+
+
+def exchange(n_row, n_col, base, factors, coupling, positions, counts, owners):
     rows_dev, cols_dev = base.shape
-    part_dev = pieces.shape[1] // (KS // n_row)
+    part_dev = coupling.shape[0]
+    smem_spec = pl.BlockSpec(memory_space=pltpu.SMEM)
     any_spec = pl.BlockSpec(memory_space=pl.ANY)
     vmem_spec = pl.BlockSpec(memory_space=pltpu.VMEM)
     dma = pltpu.SemaphoreType.DMA
@@ -410,23 +497,27 @@
             jax.ShapeDtypeStruct((TILE, PANEL), jnp.float32),
             jax.ShapeDtypeStruct((TILE, cols_dev), jnp.float32),
         ),
-        in_specs=[any_spec, vmem_spec, vmem_spec],
+        in_specs=[any_spec, any_spec, any_spec, vmem_spec, smem_spec, smem_spec],
         out_specs=(any_spec, vmem_spec, vmem_spec, vmem_spec, vmem_spec),
         scratch_shapes=[
+            pltpu.VMEM(factors.shape, factors.dtype),
+            pltpu.VMEM(coupling.shape, coupling.dtype),
             pltpu.VMEM((n_row, KS * part_dev // n_row, KS), jnp.float32),
-            pltpu.VMEM(labels.shape, jnp.int32),
+            pltpu.VMEM((n_row, 8, KS), jnp.int32),
+            pltpu.VMEM((n_row, KS * part_dev // n_row, KS), jnp.float32),
+            pltpu.VMEM((n_row, 8, KS), jnp.int32),
             pltpu.VMEM((n_row, KS * part_dev // n_row, cols_dev), jnp.bfloat16),
             pltpu.VMEM((n_row, KS * part_dev // n_row, cols_dev), jnp.bfloat16),
             pltpu.VMEM((n_col, TILE, cols_dev), jnp.float32),
             pltpu.VMEM((n_col // 2, TILE, cols_dev), jnp.float32),
             pltpu.VMEM((n_col // 2, TILE, cols_dev), jnp.float32),
-            dma((n_row,)),
-            dma((n_row,)),
+            dma((n_row, part_dev)),
+            dma((n_row, part_dev)),
             dma((n_row,)),
             dma((n_row,)),
             dma((n_col,)),
             dma((n_col,)),
-            dma((n_row,)),
+            dma((2, n_row)),
             dma((2,)),
             dma((n_col // 2,)),
             dma((n_col // 2,)),
@@ -440,11 +531,12 @@
             dma((2, n_col)),
             dma((2, n_col)),
             dma((5,)),
+            dma((2, part_dev)),
         ],
         compiler_params=pltpu.CompilerParams(
             collective_id=0, has_side_effects=True, vmem_limit_bytes=VMEM_BYTES
         ),
-    )(base, pieces, labels)
+    )(base, factors, coupling, positions, counts, owners)
 
 
 def full_dot(a, b, dims):
@@ -464,7 +556,7 @@
     return dot(a_high, b_high) + (dot(a_high, b_low) + dot(a_low, b_high))
 
 
-STEP = 4
+STEP = 8
 
 
 def cholesky_and_inverse(work, block):
@@ -594,30 +686,9 @@
 def local(base_matrix, inverse_factors, coupling, positions, counts, owners):
     n_row = lax.axis_size("row")
     n_col = lax.axis_size("col")
-    part_dev = coupling.shape[0]
-    width = KS // n_row
-    factor = jnp.einsum(
-        "pbij,pbjk->pbik", inverse_factors, coupling, preferred_element_type=jnp.float32
-    ).astype(jnp.bfloat16)
-    schur_rows = jnp.einsum("pbik,pbil->pkl", factor, factor, preferred_element_type=jnp.float32)
-    pieces = schur_rows.reshape(part_dev, n_row, width, KS).transpose(1, 0, 2, 3)
-    pieces = pieces.reshape(n_row, part_dev * width, KS)
-    within = jnp.arange(width, dtype=jnp.int32)
-    group = jnp.arange(n_row, dtype=jnp.int32)
-    usable = within[None, None, :] < counts[:, :, None]
-    place = positions.reshape(part_dev, n_row, width)
-    col_code = jnp.where(usable, group[None, :, None] * TILE + place, -1).reshape(part_dev, KS)
-    row_code = jnp.where(usable, owners[:, None, None] * TILE + place, -1)
-    row_code = row_code.transpose(1, 0, 2).reshape(n_row, 1, part_dev * width)
-    labels = jnp.concatenate(
-        [
-            jnp.broadcast_to(col_code[None], (n_row, part_dev, KS)),
-            jnp.pad(row_code, ((0, 0), (0, 0), (0, KS - part_dev * width))),
-            jnp.zeros((n_row, 7 - part_dev, KS), jnp.int32),
-        ],
-        axis=1,
+    raw, q, diag, top, tile = exchange(
+        n_row, n_col, base_matrix, inverse_factors, coupling, positions, counts, owners
     )
-    raw, q, diag, top, tile = exchange(n_row, n_col, base_matrix, pieces, labels)
     return factorise(base_matrix, raw, q, diag, top, tile)
 
 

time: 89.6 us -> 87.7 us (0.979)
  the two profiles are of different devices: /device:TPU:0 before, /device:TPU:30 now
where the time goes in v3:
time: 87.7 us; the launch traced here: 87.5 us
  Pallas kernels  85.5 us (97%)
  local copies, waits for them, and re-layouts  2.02 us (2%)
    pallas_call x1, Pallas kernels, exchange(): pl.pallas_call(functools.partial(exchange_kernel, n_row, n_col, part_dev)...  67.1 us
    pallas_call x1, Pallas kernels, factorise(): pl.pallas_call(factor_kernel, out_shape=jax.ShapeDtypeStruct(base.shape,...  18.4 us
    unnamed x6, local copies, waits for them, and re-layouts  2.02 us

profile of v3, /device:TPU:30, one launch (start us, length us, event | category | flops | bytes accessed | tf_op | source)
XLA Modules:
  0.0 87.5 jit_solution(1436904769984896016)
XLA Ops:
  0.0 0.0 copy-start
  0.0 0.7 copy-done
  0.7 0.0 copy-start.1
  0.7 0.7 copy-done.1
  1.4 0.0 copy-start.2
  1.4 0.7 copy-done.2
  2.0 67.1 %shard_map.64 = (f32[1024,256]{1,0:T(8,128)S(1)}, f32[256,512]{1,0:T(8,128)S(1)}, f32[256,256]{1,0:T(8,128)S(1)}, f32[128,256]{1,0:T(8,128)S(1)}, f32[128,512]{1,0:T(8,128)S(1)}) custom-call(f32[1024,512]{1,0:T(8,128)} %base_ref.3, bf16[4,2,512,512]{3,2,1,0:T(8,128)(2,1)} %factors_ref.1, bf16[4,2,512,256]{3,2,1,0:T(8,128)(2,1)} %coupling_ref.1, ...), custom_call_target="tpu_custom_call" | custom-call | tf_op jit(solution)/shard_map/pallas_call | solution.py:491
  69.1 18.4 %shard_map.65 = f32[1024,512]{1,0:T(8,128)} custom-call(f32[1024,512]{1,0:T(8,128)} %base_ref.3, f32[1024,256]{1,0:T(8,128)S(1)} %get-tuple-element.10.raw_ref, f32[256,512]{1,0:T(8,128)S(1)} %get-tuple-element.11.q_ref, f32[256,256]{1,0:T(8,128)S(1)} %get-tuple-element.12.diag_ref, f32[128,256]{1,0:T(8,128)S(1)} %get-tuple-element.13.top_ref, ...), custom_call_target="tpu_custom_call" | custom-call | tf_op jit(solution)/shard_map/pallas_call | solution.py:671
Async XLA Ops:
  0.0 0.7 copy-start
  0.7 0.7 copy-start.1
  1.4 0.7 copy-start.2

commit v4 on v3

--- a/solution.py
+++ b/solution.py
@@ -199,6 +199,28 @@
         label_copy(row_peer(d), r).start()
     own_label = pltpu.make_async_copy(labels.at[r], got_labels.at[r], local_sem.at[1])
     own_label.start()
+    def q_out(make, half, act):
+        if half > 0:
+            act(make(half - 1, half))
+        act(make(half + 1, half))
+
+    def q_forward(make, half, first, last):
+        @pl.when((r > half) & (r >= first) & (r < last))
+        def _():
+            make(r + 1, half).wait_recv()
+            make(r + 1, half).start()
+
+    for half in range(2):
+
+        @pl.when((r == half) & (c != 0))
+        def _():
+            own_q = pltpu.make_async_copy(
+                base_ref.at[pl.ds(0, TILE)], q_ref.at[pl.ds(half * TILE, TILE)], local_sem.at[4]
+            )
+            own_q.start()
+            own_q.wait()
+            q_out(q_copy, half, lambda copy: copy.start())
+
     own_tile = pltpu.make_async_copy(
         base_ref.at[pl.ds(c * TILE, TILE)], tile_ref, local_sem.at[3]
     )
@@ -228,6 +250,11 @@
         for d in range(1, n_row):
             piece_copy(row_peer(d), r, p).start()
 
+    @pl.when(c != 0)
+    def _():
+        for half in range(2):
+            q_forward(q_copy, half, 0, 2)
+
     own_piece = pltpu.make_async_copy(pieces.at[r], got.at[r], local_sem.at[0])
     own_piece.start()
     own_piece.wait()
@@ -269,27 +296,10 @@
 
     lax.fori_loop(1, n_row, arrive, 0)
 
-    def q_out(make, half, act):
-        if half > 0:
-            act(make(half - 1, half))
-        act(make(half + 1, half))
-
-    def q_forward(make, half, first, last):
-        @pl.when((r > half) & (r >= first) & (r < last))
-        def _():
-            make(r + 1, half).wait_recv()
-            make(r + 1, half).start()
-
-    for half in range(2):
-
-        @pl.when((r == half) & (c != 0))
-        def _():
-            own_q = pltpu.make_async_copy(
-                base_ref.at[pl.ds(0, TILE)], q_ref.at[pl.ds(half * TILE, TILE)], local_sem.at[4]
-            )
-            own_q.start()
-            own_q.wait()
-            q_out(q_copy, half, lambda copy: copy.start())
+    @pl.when(c != 0)
+    def _():
+        for half in range(2):
+            q_forward(q_copy, half, 2, n_row - 1)
 
     def gather_owner(o):
         total = jnp.zeros((TILE, cols_dev), jnp.float32)
@@ -308,11 +318,6 @@
 
     lax.fori_loop(0, pairs, gather_pair, 0)
 
-    @pl.when(c != 0)
-    def _():
-        for half in range(2):
-            q_forward(q_copy, half, 0, 2)
-
     def gather_own(j, carry):
         owner = 2 * j + parity
         gather_owner(owner)
@@ -381,10 +386,6 @@
             q_out(q_rest_copy, half, lambda copy: copy.start())
 
     for half in range(2):
-
-        @pl.when(c != 0)
-        def _():
-            q_forward(q_copy, half, 2, n_row - 1)
 
         @pl.when(c == 0)
         def _():

time: 87.7 us -> 86.8 us (0.990)
  the two profiles are of different devices: /device:TPU:30 before, /device:TPU:17 now
where the time goes in v4:
time: 86.8 us; the launch traced here: 86.6 us
  Pallas kernels  84.5 us (97%)
  local copies, waits for them, and re-layouts  2.02 us (2%)
    pallas_call x1, Pallas kernels, exchange(): pl.pallas_call(functools.partial(exchange_kernel, n_row, n_col, part_dev)...  66.2 us
    pallas_call x1, Pallas kernels, factorise(): pl.pallas_call(factor_kernel, out_shape=jax.ShapeDtypeStruct(base.shape,...  18.4 us
    unnamed x6, local copies, waits for them, and re-layouts  2.02 us

profile of v4, /device:TPU:17, one launch (start us, length us, event | category | flops | bytes accessed | tf_op | source)
XLA Modules:
  0.0 86.6 jit_solution(5990140596485674604)
XLA Ops:
  0.0 0.0 copy-start
  0.0 0.7 copy-done
  0.7 0.0 copy-start.1
  0.7 0.7 copy-done.1
  1.4 0.0 copy-start.2
  1.4 0.7 copy-done.2
  2.0 66.2 %shard_map.64 = (f32[1024,256]{1,0:T(8,128)S(1)}, f32[256,512]{1,0:T(8,128)S(1)}, f32[256,256]{1,0:T(8,128)S(1)}, f32[128,256]{1,0:T(8,128)S(1)}, f32[128,512]{1,0:T(8,128)S(1)}) custom-call(f32[1024,512]{1,0:T(8,128)} %base_ref.3, bf16[4,2,512,512]{3,2,1,0:T(8,128)(2,1)} %factors_ref.1, bf16[4,2,512,256]{3,2,1,0:T(8,128)(2,1)} %coupling_ref.1, ...), custom_call_target="tpu_custom_call" | custom-call | tf_op jit(solution)/shard_map/pallas_call | solution.py:492
  68.2 18.4 %shard_map.65 = f32[1024,512]{1,0:T(8,128)} custom-call(f32[1024,512]{1,0:T(8,128)} %base_ref.3, f32[1024,256]{1,0:T(8,128)S(1)} %get-tuple-element.10.raw_ref, f32[256,512]{1,0:T(8,128)S(1)} %get-tuple-element.11.q_ref, f32[256,256]{1,0:T(8,128)S(1)} %get-tuple-element.12.diag_ref, f32[128,256]{1,0:T(8,128)S(1)} %get-tuple-element.13.top_ref, ...), custom_call_target="tpu_custom_call" | custom-call | tf_op jit(solution)/shard_map/pallas_call | solution.py:672
Async XLA Ops:
  0.0 0.7 copy-start
  0.7 0.7 copy-start.1
  1.4 0.7 copy-start.2
